TPU v7x, 32 devices: a whole 2x2x4 slice. The times are simulated.
32 devices in a mesh: sta: 8 (over y, x, core), freq: 4 (over z).
Axes of the slice: x: 2, y: 2, z: 4, core: 2. Of those that a mesh axis runs over, the one named last changes fastest.
Arguments:
- records: bfloat16 [1024, 128, 512], P('sta', 'freq'), may hold values from -6 to 6
- available: int32 [1024, 128], P('sta', 'freq'), may hold values 0 or 1
Outputs:
- cross_gram: bfloat16 [2, 128, 1024, 1024], P(None, 'freq', 'sta')
All inputs are finite; a program needn't handle non-finite values. No bound on the sum of `available` on one device may be relied on, other than what follows from the above.
Results may differ from a plain program's by a relative error of at most 0.0056.
Values may be sent and summed in bfloat16 or wider, within the bound.
A program may use at most 192 MiB of HBM per device.

v0:
```python
import jax
import jax.numpy as jnp
from jax import lax
from jax.sharding import PartitionSpec as P

FFT_LEN = 512
BINS = 128
BAND_LO = 16


def spectra_table():
    sample_idx = jnp.arange(FFT_LEN, dtype=jnp.int32)[:, None]
    bin_idx = BAND_LO + jnp.arange(BINS, dtype=jnp.int32)[None, :]
    phase = (sample_idx * bin_idx % FFT_LEN).astype(jnp.float32) * (2.0 * jnp.pi / FFT_LEN)
    return jnp.concatenate([jnp.cos(phase), -jnp.sin(phase)], axis=1)


def gram_block(mine, other):
    count = mine.shape[3]
    both_real = jnp.einsum(
        "fas,fbs->fab", mine[:, 0], other[:, 0], preferred_element_type=jnp.float32
    )
    both_imag = jnp.einsum(
        "fas,fbs->fab", mine[:, 1], other[:, 1], preferred_element_type=jnp.float32
    )
    imag_real = jnp.einsum(
        "fas,fbs->fab", mine[:, 1], other[:, 0], preferred_element_type=jnp.float32
    )
    real_imag = jnp.einsum(
        "fas,fbs->fab", mine[:, 0], other[:, 1], preferred_element_type=jnp.float32
    )
    return jnp.stack([(both_real + both_imag) / count, (imag_real - real_imag) / count]).astype(
        jnp.bfloat16
    )


def shards(records, available):
    stations, segments, samples = records.shape
    sample_pos = jnp.arange(samples, dtype=jnp.float32)
    window_taper = 0.5 - 0.5 * jnp.cos(2.0 * jnp.pi * sample_pos / samples)
    tapered = records.astype(jnp.float32) * window_taper
    spectra = jnp.dot(
        tapered.reshape(stations * segments, samples),
        spectra_table(),
        precision=lax.Precision.HIGHEST,
        preferred_element_type=jnp.float32,
    )
    spectra = spectra.reshape(stations, segments, 2 * BINS)
    real_part = spectra[..., :BINS]
    imag_part = spectra[..., BINS:]
    power = jnp.mean(real_part * real_part + imag_part * imag_part, axis=-1, keepdims=True)
    weight = available.astype(jnp.float32)[..., None] / jnp.sqrt(power + 1e-05)
    whitened = jnp.stack([real_part * weight, imag_part * weight]).astype(jnp.bfloat16)
    whitened = jnp.transpose(whitened, (3, 0, 1, 2))
    panel = lax.all_to_all(whitened, "freq", split_axis=0, concat_axis=3, tiled=True)
    return gram_block(panel, lax.all_gather(panel, "sta", axis=2, tiled=True))


def solution(mesh):
    in_specs = (P("sta", "freq", None), P("sta", "freq"))
    out_specs = P(None, "freq", "sta", None)
    return jax.shard_map(shards, mesh=mesh, in_specs=in_specs, out_specs=out_specs, check_vma=False)
```

profile of v0, /device:TPU:1, one launch (start us, length us, event | category | flops | bytes accessed | tf_op | source)
XLA Modules:
  0.0 245.9 jit_solution(8684640684354223723)
XLA Ops:
  6.5 0.0 all-gather.2.cloned.1.call-start
  6.6 1.1 fusion.16
  7.6 3.4 %convert_multiply_fusion = f32[128,32,512]{2,1,0:T(8,128)S(1)} fusion(bf16[128,32,512]{2,1,0:T(8,128)(2,1)} %param.2, f32[512]{0:T(512)S(1)} %multiply_subtract_fusion), kind=kLoop, calls=%fused_computation.7 | loop fusion | flops 4194304 | bytes 12584960 | tf_op jit(solution)/shard_map/mul | solution.py:41
  11.1 0.0 copy-start.1
  11.1 11.3 %fusion = f32[128,32,256]{2,0,1:T(8,128)S(1)} fusion(f32[128,32,512]{2,1,0:T(8,128)S(1)} %convert_multiply_fusion, f32[512,128]{1,0:T(8,128)S(1)} %get-tuple-element.8, f32[512,128]{1,0:T(8,128)S(1)} %get-tuple-element.7), kind=kOutput, calls=%fused_computation.5 | convolution fusion | flops 6442582016 | bytes 13107200 | tf_op jit(solution)/shard_map/dot_general | solution.py:42
  22.4 0.6 add_reduce_fusion
  23.0 0.0 copy-done.1
  23.1 0.8 fusion.6
  23.9 0.2 maximum_bitcast_fusion
  24.1 2.9 %copy.12 = bf16[128,2,128,32]{2,3,1,0:T(8,128)(2,1)} copy(bf16[128,2,128,32]{0,2,3,1:T(8,128)(2,1)S(1)} %maximum_bitcast_fusion) | data formatting | bytes 4194304 | tf_op jit(solution)/shard_map/transpose | solution.py:54
  27.0 52.8 %all_to_all.18 = bf16[128,2,128,32]{2,3,1,0:T(8,128)(2,1)S(1)} all-to-all(bf16[128,2,128,32]{2,3,1,0:T(8,128)(2,1)} %copy.12), channel_id=1, replica_groups=mesh['sta'=8,'freq'=4] {'freq'}, dimensions={0} | all-to-all | bytes 4194304 | tf_op jit(solution)/shard_map/all_to_all | solution.py:55
  79.7 0.5 copy.13
  80.3 2.9 %copy.14 = bf16[32,2,128,128]{3,2,0,1:T(8,128)(2,1)} copy(bf16[32,2,128,128]{2,3,1,0:T(8,128)(2,1)S(1)} %bitcast.38) | data formatting | bytes 4194304 | tf_op jit(solution)/shard_map/all_to_all | solution.py:55
  83.2 0.0 all-gather.2.cloned.1.call-update
  83.2 0.0 copy-start
  83.2 90.8 %all-gather.2.cloned.1.call-done = bf16[32,2,1024,128]{3,2,0,1:T(8,128)(2,1)} async-done(((bf16[32,2,128,128]{3,2,0,1:T(8,128)(2,1)}), bf16[32,2,1024,128]{3,2,0,1:T(8,128)(2,1)}) %all-gather.2.cloned.1.call-update) | async-done | bytes 16777232 | tf_op jit(solution)/shard_map/all_gather | solution.py:56
  174.0 12.2 %fusion.2 = f32[32,128,1024]{2,1,0:T(8,128)} fusion(bf16[32,2,1024,128]{3,2,0,1:T(8,128)(2,1)} %all-gather.2.cloned.1.call-done, bf16[32,2,128,128]{3,2,0,1:T(8,128)(2,1)} %copy.14), kind=kOutput, calls=%fused_computation.8 | convolution fusion | flops 1073741824 | bytes 26214400 | tf_op jit(solution)/shard_map/fas,fbs->fab/dot_general | solution.py:26
  186.2 0.0 copy-done
  186.2 11.4 %fusion.3 = f32[32,128,1024]{2,1,0:T(8,128)} fusion(bf16[32,2,1024,128]{3,2,0,1:T(8,128)(2,1)} %all-gather.2.cloned.1.call-done, bf16[32,2,128,128]{3,2,0,1:T(8,128)(2,1)S(1)} %copy-done), kind=kOutput, calls=%fused_computation.9 | convolution fusion | flops 1073741824 | bytes 26214400 | tf_op jit(solution)/shard_map/fas,fbs->fab/dot_general | solution.py:20
  197.7 13.8 %fusion.5 = bf16[1,32,128,1024]{3,2,1,0:T(8,128)(2,1)} fusion(f32[32,128,1024]{2,1,0:T(8,128)} %fusion.2, bf16[32,2,1024,128]{3,2,0,1:T(8,128)(2,1)} %all-gather.2.cloned.1.call-done, bf16[32,2,128,128]{3,2,0,1:T(8,128)(2,1)S(1)} %copy-done), kind=kOutput, calls=%fused_computation.11 | convolution fusion | flops 1086324736 | bytes 34603008 | tf_op jit(solution)/shard_map/fas,fbs->fab/dot_general | solution.py:29
  211.5 13.8 %fusion.4 = bf16[1,32,128,1024]{3,2,1,0:T(8,128)(2,1)} fusion(f32[32,128,1024]{2,1,0:T(8,128)} %fusion.3, bf16[32,2,1024,128]{3,2,0,1:T(8,128)(2,1)} %all-gather.2.cloned.1.call-done, bf16[32,2,128,128]{3,2,0,1:T(8,128)(2,1)S(1)} %copy-done), kind=kOutput, calls=%fused_computation.10 | convolution fusion | flops 1086324736 | bytes 34603008 | tf_op jit(solution)/shard_map/fas,fbs->fab/dot_general | solution.py:23
  225.3 13.8 %pad_maximum_fusion = bf16[2,32,128,1024]{3,2,1,0:T(8,128)(2,1)} fusion(bf16[1,32,128,1024]{3,2,1,0:T(8,128)(2,1)} %fusion.5, bf16[1,32,128,1024]{3,2,1,0:T(8,128)(2,1)} %fusion.4), kind=kLoop, calls=%fused_computation | loop fusion | flops 8388608 | bytes 33554432 | tf_op jit(solution)/shard_map/stack | solution.py:32
  (3 shorter events, 0.1 us)
Async XLA Ops:
  6.5 167.5 %all-gather.2.cloned.1.call-start = ((), (), s32[]{:S(2)}) async-start(), calls=%async_computation.1 | async-start | bytes 18874368 | tf_op jit(solution)/shard_map/all_gather | solution.py:56
  11.1 11.9 %copy-start.1 = (s32[128,32]{0,1:T(8,128)S(1)}, s32[128,32]{0,1:T(8,128)}, u32[]{:S(2)}) copy-start(s32[128,32]{0,1:T(8,128)} %param.3) | copy-start | bytes 49156
  83.2 103.0 %copy-start = (bf16[32,2,128,128]{3,2,0,1:T(8,128)(2,1)S(1)}, bf16[32,2,128,128]{3,2,0,1:T(8,128)(2,1)}, u32[]{:S(2)}) copy-start(bf16[32,2,128,128]{3,2,0,1:T(8,128)(2,1)} %copy.14) | copy-start | bytes 6291460
Sparse Core Ops, SparseCore 0:
  83.3 90.6 all-gather.1
where the time goes:
time: 246 us
  waiting for transfers between devices  90.8 us (37%)
  matrix products  62.6 us (25%)
  blocking collectives  52.8 us (21%)
  other arithmetic  20 us (8%)
  between operations  13.5 us (5%)
  local copies, waits for them, and re-layouts  6.36 us (3%)
    all_gather x1, waiting for transfers between devices, shards(): return gram_block(panel, lax.all_gather(panel, 'sta', axis=2, tiled=True))  90.8 us
    all_to_all x1, blocking collectives, shards(): lax.all_to_all(whitened, 'freq', split_axis=0, concat_axis=3, tiled=True)  52.8 us
    another operation x1, other arithmetic, gram_block(): jnp.stack([(both_real + both_imag) / count, (imag_real - real_imag) / cou...  13.8 us
    dot_general x1, matrix products, gram_block(): jnp.einsum('fas,fbs->fab', mine[:, 1], other[:, 1], preferred_element_typ...  13.8 us
    dot_general x1, matrix products, gram_block(): jnp.einsum('fas,fbs->fab', mine[:, 0], other[:, 1], preferred_element_typ...  13.8 us
    dot_general x1, matrix products, gram_block(): jnp.einsum('fas,fbs->fab', mine[:, 1], other[:, 0], preferred_element_typ...  12.2 us
    dot_general x1, matrix products, gram_block(): jnp.einsum('fas,fbs->fab', mine[:, 0], other[:, 0], preferred_element_typ...  11.4 us
    dot_general x1, matrix products, shards(): jnp.dot(tapered.reshape(stations * segments, samples), spectra_table(), p...  11.3 us
  transfers between devices with their start and end apart: 1, of which 1 were waited for; matrix products, arithmetic and copies ran while one was open for 0% of the time, Pallas kernels for 0%

commit v1 on v0

v1 whole, which is shorter than its diff:
```python
import functools

import jax
import jax.numpy as jnp
import ml_dtypes
import numpy as np
from jax import lax
from jax.experimental import pallas as pl
from jax.experimental.pallas import tpu as pltpu
from jax.sharding import PartitionSpec as P

FFT_LEN = 512
BINS = 128
BAND_LO = 16
PARTS = 2
MESH = pl.DeviceIdType.MESH
MIB = 1 << 20


def spectra_tables():
    t = np.arange(FFT_LEN)
    window = 0.5 - 0.5 * np.cos(2.0 * np.pi * t / FFT_LEN)
    phase = (np.arange(BAND_LO, BAND_LO + BINS)[:, None] * t[None, :] % FFT_LEN) * (2.0 * np.pi / FFT_LEN)
    table = np.concatenate([np.cos(phase), -np.sin(phase)], axis=0) * window
    high = table.astype(ml_dtypes.bfloat16)
    low = (table - high.astype(np.float64)).astype(ml_dtypes.bfloat16)
    return high, low


def exchange_kernel(
    n_sta, n_freq,
    records, avail, high, low, gathered,
    rec, wide, spread, own, rec_sem, keep_sem, zsend, zrecv, send, recv,
):
    me = lax.axis_index("sta")
    z = lax.axis_index("freq")
    stations, part_segs = rec.shape[1], rec.shape[2]
    rows = 2 * part_segs
    bins = BINS // n_freq
    mask_bits = [1 << k for k in range(n_sta.bit_length() - 1)]
    far_bits = mask_bits[1:]

    loads = []
    for part in range(PARTS):
        load = pltpu.make_async_copy(
            records.at[:, pl.ds(part * part_segs, part_segs), :], rec.at[part], rec_sem.at[part]
        )
        load.start()
        loads.append(load)

    barrier = pltpu.get_barrier_semaphore()
    for bit in mask_bits:
        pl.semaphore_signal(barrier, inc=1, device_id=(me ^ bit, z), device_id_type=MESH)
    for step in range(1, n_freq):
        pl.semaphore_signal(barrier, inc=1, device_id=(me, z ^ step), device_id_type=MESH)

    def transform(part):
        loads[part].wait()

        def widen(block, carry):
            first = pl.multiple_of(block * 16, 16)
            for col in range(FFT_LEN // 128):
                values = rec[part, pl.ds(first, 16), :, pl.ds(col * 128, 128)]
                wide[col, pl.ds(pl.multiple_of(first * part_segs, 256), 16 * part_segs), :] = (
                    values.astype(jnp.float32).reshape(16 * part_segs, 128)
                )
            return carry

        lax.fori_loop(0, stations // 16, widen, 0)

        for pair in range(part_segs // 2):
            pieces = []
            for seg in (2 * pair, 2 * pair + 1):
                pieces.append(jnp.concatenate(
                    [wide[col, pl.ds(seg, stations, stride=part_segs), :] for col in range(FFT_LEN // 128)], axis=1
                ))
            x = jnp.concatenate(pieces, axis=0).astype(jnp.bfloat16)
            contract = (((1,), (1,)), ((), ()))
            spectra = lax.dot_general(high[...], x, contract, preferred_element_type=jnp.float32)
            spectra += lax.dot_general(low[...], x, contract, preferred_element_type=jnp.float32)
            power = jnp.sum(spectra * spectra, axis=0, keepdims=True) * (1.0 / BINS)
            for k, seg in enumerate((2 * pair, 2 * pair + 1)):
                lanes = slice(k * stations, (k + 1) * stations)
                usable = avail[pl.ds(part * part_segs + seg, 1), :]
                weight = usable / jnp.sqrt(power[:, lanes] + 1e-05)
                white = spectra[:, lanes] * weight
                spread[pl.ds(seg, BINS, stride=rows), :] = white[:BINS]
                spread[pl.ds(part_segs + seg, BINS, stride=rows), :] = white[BINS:]

        for dest in range(n_freq):
            block = spread[dest * bins * rows:(dest + 1) * bins * rows, :]
            own[dest, part] = block.astype(jnp.bfloat16).reshape(bins, rows, 128)

    def orders(part):
        return far_bits if part % 2 == 0 else far_bits[::-1]

    def piece(step, part, mask):
        return gathered.at[me ^ mask, z ^ step, part]

    def forward(step, part, mask, bit):
        src = own.at[z, part] if mask == 0 and step == 0 else piece(step, part, mask)
        return pltpu.make_async_remote_copy(
            src_ref=src, dst_ref=piece(step, part, mask),
            send_sem=send.at[step * PARTS + part, mask ^ bit], recv_sem=recv.at[step * PARTS + part, mask ^ bit],
            device_id=(me ^ bit, z), device_id_type=MESH,
        )

    def arrival(step, part, mask):
        here = piece(step, part, mask)
        return pltpu.make_async_remote_copy(
            src_ref=here, dst_ref=here,
            send_sem=send.at[step * PARTS + part, mask], recv_sem=recv.at[step * PARTS + part, mask],
            device_id=(me ^ (mask & -mask), z), device_id_type=MESH,
        )

    def cross(step, part):
        return pltpu.make_async_remote_copy(
            src_ref=own.at[z ^ step, part], dst_ref=gathered.at[me, z, part],
            send_sem=zsend.at[step * PARTS + part], recv_sem=zrecv.at[step * PARTS + part],
            device_id=(me, z ^ step), device_id_type=MESH,
        )

    def crossed(step, part):
        here = piece(step, part, 0)
        return pltpu.make_async_remote_copy(
            src_ref=here, dst_ref=here,
            send_sem=zsend.at[step * PARTS + part], recv_sem=zrecv.at[step * PARTS + part],
            device_id=(me, z ^ step), device_id_type=MESH,
        )

    started = []

    def push(step, part, mask):
        order = orders(part)
        last = max([order.index(bit) for bit in order if mask & bit], default=-1)
        for bit in order[last + 1:] + [1]:
            copy = forward(step, part, mask, bit)
            copy.start()
            started.append(copy)

    keeps = []
    for part in range(PARTS):
        transform(part)
        if part == 0:
            pl.semaphore_wait(barrier, len(mask_bits) + n_freq - 1)
        push(0, part, 0)
        for step in range(1, n_freq):
            copy = cross(step, part)
            copy.start()
            started.append(copy)
        keep = pltpu.make_async_copy(own.at[z, part], gathered.at[me, z, part], keep_sem.at[part])
        keep.start()
        keeps.append(keep)

    far_masks = [mask for mask in range(2, n_sta, 2)]
    count = n_freq * PARTS
    depth = len(far_bits)
    for turn in range(PARTS, count + depth + 1):
        for lag in range(depth + 1):
            index = turn - lag
            if lag == 0 and index < count:
                step, part = divmod(index, PARTS)
                crossed(step, part).wait_recv()
                push(step, part, 0)
            lower = 0 if turn == PARTS else index
            for slot in range(lower, index + 1):
                if lag > 0 and 0 <= slot < count:
                    step, part = divmod(slot, PARTS)
                    for mask in far_masks:
                        if bin(mask).count("1") == lag:
                            arrival(step, part, mask).wait_recv()
                            push(step, part, mask)

    for slot in range(count):
        step, part = divmod(slot, PARTS)
        for mask in range(1, n_sta, 2):
            arrival(step, part, mask).wait_recv()
    for keep in keeps:
        keep.wait()
    for copy in started:
        copy.wait_send()


def gram_kernel(per_step, scale, panel, out):
    me = lax.axis_index("sta")
    n_sta, n_freq, parts, _, rows, _ = panel.shape
    half = rows // 2
    places = [(z, part) for z in range(n_freq) for part in range(parts)]
    for b in range(per_step):
        plain, turned = [], []
        for z, part in places:
            block = panel[me, z, part, b] * scale
            plain.append(block)
            turned += [block[half:], -block[:half]]
        mine = jnp.concatenate([jnp.concatenate(plain, axis=0), jnp.concatenate(turned, axis=0)], axis=1)
        every = jnp.concatenate(
            [jnp.concatenate([panel[j, z, part, b] for z, part in places], axis=0) for j in range(n_sta)], axis=1
        )
        gram = lax.dot_general(mine, every, (((0,), (0,)), ((), ())), preferred_element_type=jnp.float32)
        gram = gram.astype(jnp.bfloat16)
        stations = out.shape[2]
        out[0, b] = gram[:stations]
        out[1, b] = gram[stations:]


def shards(n_sta, n_freq, records, available):
    stations, segments, samples = records.shape
    part_segs = segments // PARTS
    rows = 2 * part_segs
    bins = BINS // n_freq
    avail = available.astype(jnp.float32).T
    high, low = spectra_tables()
    vmem = pl.BlockSpec(memory_space=pltpu.VMEM)
    count = n_freq * PARTS
    gathered = pl.pallas_call(
        functools.partial(exchange_kernel, n_sta, n_freq),
        out_shape=jax.ShapeDtypeStruct((n_sta, n_freq, PARTS, bins, rows, stations), jnp.bfloat16),
        in_specs=[pl.BlockSpec(memory_space=pl.ANY), vmem, vmem, vmem],
        out_specs=pl.BlockSpec(memory_space=pl.ANY),
        scratch_shapes=[
            pltpu.VMEM((PARTS, stations, part_segs, samples), jnp.bfloat16),
            pltpu.VMEM((samples // 128, stations * part_segs, 128), jnp.float32),
            pltpu.VMEM((BINS * rows, stations), jnp.float32),
            pltpu.VMEM((n_freq, PARTS, bins, rows, stations), jnp.bfloat16),
            pltpu.SemaphoreType.DMA((PARTS,)),
            pltpu.SemaphoreType.DMA((PARTS,)),
            pltpu.SemaphoreType.DMA((count,)),
            pltpu.SemaphoreType.DMA((count,)),
            pltpu.SemaphoreType.DMA((count, n_sta)),
            pltpu.SemaphoreType.DMA((count, n_sta)),
        ],
        compiler_params=pltpu.CompilerParams(
            collective_id=0, has_side_effects=True, vmem_limit_bytes=20 * MIB
        ),
        name="spectra_exchange",
    )(records, avail, jnp.asarray(high), jnp.asarray(low))

    per_step = 4
    scale = 1.0 / (segments * n_freq)
    return pl.pallas_call(
        functools.partial(gram_kernel, per_step, scale),
        out_shape=jax.ShapeDtypeStruct((2, bins, stations, stations * n_sta), jnp.bfloat16),
        grid=(bins // per_step,),
        in_specs=[pl.BlockSpec((n_sta, n_freq, PARTS, per_step, rows, stations), lambda i: (0, 0, 0, i, 0, 0))],
        out_specs=pl.BlockSpec((2, per_step, stations, stations * n_sta), lambda i: (0, i, 0, 0)),
        compiler_params=pltpu.CompilerParams(vmem_limit_bytes=40 * MIB),
        name="gram",
    )(gathered)


def solution(mesh):
    in_specs = (P("sta", "freq", None), P("sta", "freq"))
    out_specs = P(None, "freq", "sta", None)
    body = functools.partial(shards, mesh.shape["sta"], mesh.shape["freq"])
    return jax.shard_map(body, mesh=mesh, in_specs=in_specs, out_specs=out_specs, check_vma=False)
```

time: 246 us -> 111 us (0.45)
  Pallas kernels: 0 us -> 100 us
  waiting for transfers between devices: 90.8 us -> 0 us
  matrix products: 62.6 us -> 0 us
  blocking collectives: 52.8 us -> 0 us
  other arithmetic: 20 us -> 0.72 us
  between operations: 13.5 us -> 0.02 us
  local copies, waits for them, and re-layouts: 6.36 us -> 9.81 us
    pallas_call x0 -> x2, Pallas kernels: none -> 100 us  [the longest x1 84.3 us: shards(): pl.pallas_call(functools.partial(exchange_kernel, n_sta, n_freq), out_sha...]
    all_gather x1 -> x0, waiting for transfers between devices: 90.8 us -> none  [shards(): return gram_block(panel, lax.all_gather(panel, 'sta', axis=2, tiled=True))]
    dot_general x5 -> x0, matrix products: 62.6 us -> none  [the longest x1 13.8 us: gram_block(): jnp.einsum('fas,fbs->fab', mine[:, 1], other[:, 1], preferred_element_typ...]
    all_to_all x1 -> x0, blocking collectives: 52.8 us -> none  [shards(): lax.all_to_all(whitened, 'freq', split_axis=0, concat_axis=3, tiled=True)]
    another operation x2 -> x0, other arithmetic: 14.6 us -> none  [the longest x1 13.8 us: gram_block(): jnp.stack([(both_real + both_imag) / count, (imag_real - real_imag) / cou...]
    unnamed x4 -> x8, local copies, waits for them, and re-layouts: 0.01 us -> 9.81 us
    all_to_all x2 -> x0, local copies, waits for them, and re-layouts: 3.45 us -> none  [shards(): lax.all_to_all(whitened, 'freq', split_axis=0, concat_axis=3, tiled=True)]
    mul x1 -> x0, other arithmetic: 3.43 us -> none  [shards(): tapered = records.astype(jnp.float32) * window_taper]
  transfers between devices with their start and end apart: 1 -> 0, of which waited for: 1 -> 0; matrix products, arithmetic and copies ran while one was open for 0% -> 0% of each run, Pallas kernels for 0% -> 0%
where the time goes in v1:
time: 111 us
  Pallas kernels  100 us (90%)
  local copies, waits for them, and re-layouts  9.81 us (9%)
    pallas_call x1, Pallas kernels, shards(): pl.pallas_call(functools.partial(exchange_kernel, n_sta, n_freq), out_sha...  84.3 us
    pallas_call x1, Pallas kernels, shards(): pl.pallas_call(functools.partial(gram_kernel, per_step, scale), out_shape...  16.1 us
    unnamed x8, local copies, waits for them, and re-layouts  9.81 us

profile of v1, /device:TPU:1, one launch (start us, length us, event | category | flops | bytes accessed | tf_op | source)
XLA Modules:
  0.0 110.9 jit_solution(11932037529842460844)
XLA Ops:
  0.0 0.7 convert_bitcast_fusion.avail
  0.7 0.0 copy-start.1
  0.7 2.2 %copy-done.1 = bf16[128,32,512]{2,1,0:T(8,128)(2,1)S(1)} copy-done((bf16[128,32,512]{2,1,0:T(8,128)(2,1)S(1)}, bf16[128,32,512]{2,1,0:T(8,128)(2,1)}, u32[]{:S(2)}) %copy-start.1) | copy-done | bytes 4194328
  2.9 0.0 copy-start.2
  2.9 0.9 copy-done.2
  3.9 0.0 copy-start.3
  3.9 0.9 copy-done.3
  4.8 84.3 %spectra_exchange.1.panel = bf16[8,4,2,32,32,128]{5,4,3,2,1,0:T(8,128)(2,1)S(1)} custom-call(bf16[128,32,512]{2,1,0:T(8,128)(2,1)S(1)} %copy-done.1, f32[32,128]{1,0:T(8,128)S(1)} %convert_bitcast_fusion.avail, bf16[256,512]{1,0:T(8,128)(2,1)S(1)} %copy-done.3, bf16[256,512]{1,0:T(8,128)(2,1)S(1)} %copy-done.2), custom_call_target="tpu_custom_call" | custom-call | tf_op jit(solution)/shard_map/spectra_exchange/pallas_call | solution.py:215
  89.1 0.0 copy-start
  89.1 5.7 %copy-done = bf16[8,4,2,32,32,128]{5,4,3,2,1,0:T(8,128)(2,1)} copy-done((bf16[8,4,2,32,32,128]{5,4,3,2,1,0:T(8,128)(2,1)}, bf16[8,4,2,32,32,128]{5,4,3,2,1,0:T(8,128)(2,1)S(1)}, u32[]{:S(2)}) %copy-start) | copy-done | bytes 16777240
  94.8 16.1 %gram.1 = bf16[2,32,128,1024]{3,2,1,0:T(8,128)(2,1)} custom-call(bf16[8,4,2,32,32,128]{5,4,3,2,1,0:T(8,128)(2,1)} %copy-done), custom_call_target="tpu_custom_call" | custom-call | tf_op jit(solution)/shard_map/gram/pallas_call | solution.py:240
Async XLA Ops:
  0.7 2.2 %copy-start.1 = (bf16[128,32,512]{2,1,0:T(8,128)(2,1)S(1)}, bf16[128,32,512]{2,1,0:T(8,128)(2,1)}, u32[]{:S(2)}) copy-start(bf16[128,32,512]{2,1,0:T(8,128)(2,1)} %records.1) | copy-start | bytes 12582916
  2.9 0.9 copy-start.2
  3.9 0.9 copy-start.3
  89.1 5.7 %copy-start = (bf16[8,4,2,32,32,128]{5,4,3,2,1,0:T(8,128)(2,1)}, bf16[8,4,2,32,32,128]{5,4,3,2,1,0:T(8,128)(2,1)S(1)}, u32[]{:S(2)}) copy-start(bf16[8,4,2,32,32,128]{5,4,3,2,1,0:T(8,128)(2,1)S(1)} %spectra_exchange.1.panel) | copy-start | bytes 50331652

commit v2 on v1

--- a/solution.py
+++ b/solution.py
@@ -12,7 +12,9 @@
 FFT_LEN = 512
 BINS = 128
 BAND_LO = 16
-PARTS = 2
+PARTS = 4
+TERMS = 3
+LOADS = 2
 MESH = pl.DeviceIdType.MESH
 MIB = 1 << 20
 
@@ -22,31 +24,34 @@
     window = 0.5 - 0.5 * np.cos(2.0 * np.pi * t / FFT_LEN)
     phase = (np.arange(BAND_LO, BAND_LO + BINS)[:, None] * t[None, :] % FFT_LEN) * (2.0 * np.pi / FFT_LEN)
     table = np.concatenate([np.cos(phase), -np.sin(phase)], axis=0) * window
-    high = table.astype(ml_dtypes.bfloat16)
-    low = (table - high.astype(np.float64)).astype(ml_dtypes.bfloat16)
-    return high, low
+    terms = []
+    for _ in range(TERMS):
+        terms.append(table.astype(ml_dtypes.bfloat16))
+        table = table - terms[-1].astype(np.float64)
+    return np.concatenate(terms, axis=0)
 
 
 def exchange_kernel(
     n_sta, n_freq,
-    records, avail, high, low, gathered,
-    rec, wide, spread, own, rec_sem, keep_sem, zsend, zrecv, send, recv,
+    records, available, table, gathered,
+    rec, avail, terms, wide, spread, own, rec_sem, keep_sem, zsend, zrecv, send, recv,
 ):
     me = lax.axis_index("sta")
     z = lax.axis_index("freq")
-    stations, part_segs = rec.shape[1], rec.shape[2]
+    stations, load_segs = rec.shape[1], rec.shape[2]
+    part_segs = load_segs * LOADS // PARTS
     rows = 2 * part_segs
     bins = BINS // n_freq
     mask_bits = [1 << k for k in range(n_sta.bit_length() - 1)]
     far_bits = mask_bits[1:]
 
-    loads = []
-    for part in range(PARTS):
-        load = pltpu.make_async_copy(
-            records.at[:, pl.ds(part * part_segs, part_segs), :], rec.at[part], rec_sem.at[part]
-        )
+    loads = [pltpu.make_async_copy(table, terms, rec_sem.at[LOADS])]
+    loads.append(pltpu.make_async_copy(available, avail, rec_sem.at[LOADS + 1]))
+    for k in range(LOADS):
+        source = records.at[:, pl.ds(k * load_segs, load_segs), :]
+        loads.append(pltpu.make_async_copy(source, rec.at[k], rec_sem.at[k]))
+    for load in loads:
         load.start()
-        loads.append(load)
 
     barrier = pltpu.get_barrier_semaphore()
     for bit in mask_bits:
@@ -54,34 +59,37 @@
     for step in range(1, n_freq):
         pl.semaphore_signal(barrier, inc=1, device_id=(me, z ^ step), device_id_type=MESH)
 
-    def transform(part):
-        loads[part].wait()
-
-        def widen(block, carry):
+    def widen(k):
+        def some(block, carry):
             first = pl.multiple_of(block * 16, 16)
             for col in range(FFT_LEN // 128):
-                values = rec[part, pl.ds(first, 16), :, pl.ds(col * 128, 128)]
-                wide[col, pl.ds(pl.multiple_of(first * part_segs, 256), 16 * part_segs), :] = (
-                    values.astype(jnp.float32).reshape(16 * part_segs, 128)
+                values = rec[k, pl.ds(first, 16), :, pl.ds(col * 128, 128)]
+                wide[col, pl.ds(pl.multiple_of(first * load_segs, 256), 16 * load_segs), :] = (
+                    values.astype(jnp.float32).reshape(16 * load_segs, 128)
                 )
             return carry
 
-        lax.fori_loop(0, stations // 16, widen, 0)
-
+        lax.fori_loop(0, stations // 16, some, 0)
+
+    def transform(part):
+        offset = part * part_segs % load_segs
         for pair in range(part_segs // 2):
             pieces = []
             for seg in (2 * pair, 2 * pair + 1):
                 pieces.append(jnp.concatenate(
-                    [wide[col, pl.ds(seg, stations, stride=part_segs), :] for col in range(FFT_LEN // 128)], axis=1
+                    [wide[col, pl.ds(offset + seg, stations, stride=load_segs), :] for col in range(FFT_LEN // 128)],
+                    axis=1,
                 ))
             x = jnp.concatenate(pieces, axis=0).astype(jnp.bfloat16)
             contract = (((1,), (1,)), ((), ()))
-            spectra = lax.dot_general(high[...], x, contract, preferred_element_type=jnp.float32)
-            spectra += lax.dot_general(low[...], x, contract, preferred_element_type=jnp.float32)
+            sums = lax.dot_general(terms[...], x, contract, preferred_element_type=jnp.float32)
+            spectra = sums[(TERMS - 1) * 2 * BINS:]
+            for term in range(TERMS - 2, -1, -1):
+                spectra = spectra + sums[term * 2 * BINS:(term + 1) * 2 * BINS]
             power = jnp.sum(spectra * spectra, axis=0, keepdims=True) * (1.0 / BINS)
             for k, seg in enumerate((2 * pair, 2 * pair + 1)):
                 lanes = slice(k * stations, (k + 1) * stations)
-                usable = avail[pl.ds(part * part_segs + seg, 1), :]
+                usable = avail[pl.ds(part * part_segs + seg, 1), :].astype(jnp.float32)
                 weight = usable / jnp.sqrt(power[:, lanes] + 1e-05)
                 white = spectra[:, lanes] * weight
                 spread[pl.ds(seg, BINS, stride=rows), :] = white[:BINS]
@@ -140,6 +148,12 @@
 
     keeps = []
     for part in range(PARTS):
+        if part == 0:
+            loads[0].wait()
+            loads[1].wait()
+        if part % (PARTS // LOADS) == 0:
+            loads[2 + part * LOADS // PARTS].wait()
+            widen(part * LOADS // PARTS)
         transform(part)
         if part == 0:
             pl.semaphore_wait(barrier, len(mask_bits) + n_freq - 1)
@@ -185,22 +199,27 @@
     me = lax.axis_index("sta")
     n_sta, n_freq, parts, _, rows, _ = panel.shape
     half = rows // 2
+    first = pl.program_id(0) * per_step
     places = [(z, part) for z in range(n_freq) for part in range(parts)]
+    stations = out.shape[2]
+    wide = 2 * stations
     for b in range(per_step):
         plain, turned = [], []
         for z, part in places:
-            block = panel[me, z, part, b] * scale
+            block = panel[me, z, part, first + b].astype(jnp.float32) * scale
             plain.append(block)
             turned += [block[half:], -block[:half]]
         mine = jnp.concatenate([jnp.concatenate(plain, axis=0), jnp.concatenate(turned, axis=0)], axis=1)
-        every = jnp.concatenate(
-            [jnp.concatenate([panel[j, z, part, b] for z, part in places], axis=0) for j in range(n_sta)], axis=1
-        )
-        gram = lax.dot_general(mine, every, (((0,), (0,)), ((), ())), preferred_element_type=jnp.float32)
-        gram = gram.astype(jnp.bfloat16)
-        stations = out.shape[2]
-        out[0, b] = gram[:stations]
-        out[1, b] = gram[stations:]
+        mine = mine.T.astype(jnp.bfloat16)
+        for j in range(0, n_sta, 2):
+            other = jnp.concatenate(
+                [jnp.concatenate([panel[j + k, z, part, first + b] for z, part in places], axis=0) for k in (0, 1)],
+                axis=1,
+            )
+            gram = jnp.dot(mine, other, preferred_element_type=jnp.float32).astype(jnp.bfloat16)
+            columns = slice(j * stations, j * stations + wide)
+            out[0, b, :, columns] = gram[:stations]
+            out[1, b, :, columns] = gram[stations:]
 
 
 def shards(n_sta, n_freq, records, available):
@@ -208,21 +227,22 @@
     part_segs = segments // PARTS
     rows = 2 * part_segs
     bins = BINS // n_freq
-    avail = available.astype(jnp.float32).T
-    high, low = spectra_tables()
-    vmem = pl.BlockSpec(memory_space=pltpu.VMEM)
+    operands = [records, available.T, jnp.asarray(spectra_tables())]
+    operands = [pltpu.with_memory_space_constraint(operand, pltpu.HBM) for operand in operands]
     count = n_freq * PARTS
     gathered = pl.pallas_call(
         functools.partial(exchange_kernel, n_sta, n_freq),
         out_shape=jax.ShapeDtypeStruct((n_sta, n_freq, PARTS, bins, rows, stations), jnp.bfloat16),
-        in_specs=[pl.BlockSpec(memory_space=pl.ANY), vmem, vmem, vmem],
+        in_specs=[pl.BlockSpec(memory_space=pltpu.HBM)] * len(operands),
         out_specs=pl.BlockSpec(memory_space=pl.ANY),
         scratch_shapes=[
-            pltpu.VMEM((PARTS, stations, part_segs, samples), jnp.bfloat16),
-            pltpu.VMEM((samples // 128, stations * part_segs, 128), jnp.float32),
+            pltpu.VMEM((LOADS, stations, segments // LOADS, samples), jnp.bfloat16),
+            pltpu.VMEM((segments, stations), jnp.int32),
+            pltpu.VMEM((TERMS * 2 * BINS, samples), jnp.bfloat16),
+            pltpu.VMEM((samples // 128, stations * segments // LOADS, 128), jnp.float32),
             pltpu.VMEM((BINS * rows, stations), jnp.float32),
             pltpu.VMEM((n_freq, PARTS, bins, rows, stations), jnp.bfloat16),
-            pltpu.SemaphoreType.DMA((PARTS,)),
+            pltpu.SemaphoreType.DMA((LOADS + 2,)),
             pltpu.SemaphoreType.DMA((PARTS,)),
             pltpu.SemaphoreType.DMA((count,)),
             pltpu.SemaphoreType.DMA((count,)),
@@ -230,10 +250,10 @@
             pltpu.SemaphoreType.DMA((count, n_sta)),
         ],
         compiler_params=pltpu.CompilerParams(
-            collective_id=0, has_side_effects=True, vmem_limit_bytes=20 * MIB
+            collective_id=0, has_side_effects=True, vmem_limit_bytes=18 * MIB
         ),
         name="spectra_exchange",
-    )(records, avail, jnp.asarray(high), jnp.asarray(low))
+    )(*operands)
 
     per_step = 4
     scale = 1.0 / (segments * n_freq)
@@ -241,9 +261,9 @@
         functools.partial(gram_kernel, per_step, scale),
         out_shape=jax.ShapeDtypeStruct((2, bins, stations, stations * n_sta), jnp.bfloat16),
         grid=(bins // per_step,),
-        in_specs=[pl.BlockSpec((n_sta, n_freq, PARTS, per_step, rows, stations), lambda i: (0, 0, 0, i, 0, 0))],
+        in_specs=[pl.BlockSpec(memory_space=pltpu.VMEM)],
         out_specs=pl.BlockSpec((2, per_step, stations, stations * n_sta), lambda i: (0, i, 0, 0)),
-        compiler_params=pltpu.CompilerParams(vmem_limit_bytes=40 * MIB),
+        compiler_params=pltpu.CompilerParams(vmem_limit_bytes=12 * MIB),
         name="gram",
     )(gathered)
 

time: 111 us -> 92.1 us (0.83)
  local copies, waits for them, and re-layouts: 9.81 us -> 0 us
  Pallas kernels: 100 us -> 91.5 us
    unnamed x8 -> x0, local copies, waits for them, and re-layouts: 9.81 us -> none
    pallas_call x1, Pallas kernels: 16.1 us -> 9.19 us  [shards(): pl.pallas_call(functools.partial(gram_kernel, per_step, scale), out_shape...]
    pallas_call x1, Pallas kernels: 84.3 us -> 82.3 us  [shards(): pl.pallas_call(functools.partial(exchange_kernel, n_sta, n_freq), out_sha...]
where the time goes in v2:
time: 92.1 us; the launch traced here: 91.5 us
  Pallas kernels  91.5 us (99%)
    pallas_call x1, Pallas kernels, shards(): pl.pallas_call(functools.partial(exchange_kernel, n_sta, n_freq), out_sha...  82.3 us
    pallas_call x1, Pallas kernels, shards(): pl.pallas_call(functools.partial(gram_kernel, per_step, scale), out_shape...  9.19 us

profile of v2, /device:TPU:1, one launch (start us, length us, event | category | flops | bytes accessed | tf_op | source)
XLA Modules:
  0.0 91.5 jit_solution(8598076037978780525)
XLA Ops:
  0.0 82.3 %spectra_exchange.1.panel = bf16[8,4,4,32,16,128]{5,4,3,2,1,0:T(8,128)(2,1)S(1)} custom-call(bf16[128,32,512]{2,1,0:T(8,128)(2,1)} %records.1, s32[32,128]{1,0:T(8,128)} %bitcast.1, bf16[768,512]{1,0:T(8,128)(2,1)} %constant.2.clone.table), custom_call_target="tpu_custom_call" | custom-call | tf_op jit(solution)/shard_map/spectra_exchange/pallas_call | solution.py:233
  82.3 9.2 %gram.1 = bf16[2,32,128,1024]{3,2,1,0:T(8,128)(2,1)} custom-call(bf16[8,4,4,32,16,128]{5,4,3,2,1,0:T(8,128)(2,1)S(1)} %spectra_exchange.1.panel), custom_call_target="tpu_custom_call" | custom-call | tf_op jit(solution)/shard_map/gram/pallas_call | solution.py:260

commit v3 on v2

--- a/solution.py
+++ b/solution.py
@@ -15,6 +15,8 @@
 PARTS = 4
 TERMS = 3
 LOADS = 2
+AHEAD = 2
+Z_AHEAD = 6
 MESH = pl.DeviceIdType.MESH
 MIB = 1 << 20
 
@@ -146,6 +148,11 @@
             copy.start()
             started.append(copy)
 
+    def launch(step, part):
+        copy = cross(step, part)
+        copy.start()
+        started.append(copy)
+
     keeps = []
     for part in range(PARTS):
         if part == 0:
@@ -158,10 +165,7 @@
         if part == 0:
             pl.semaphore_wait(barrier, len(mask_bits) + n_freq - 1)
         push(0, part, 0)
-        for step in range(1, n_freq):
-            copy = cross(step, part)
-            copy.start()
-            started.append(copy)
+        launch(1, part)
         keep = pltpu.make_async_copy(own.at[z, part], gathered.at[me, z, part], keep_sem.at[part])
         keep.start()
         keeps.append(keep)
@@ -169,21 +173,26 @@
     far_masks = [mask for mask in range(2, n_sta, 2)]
     count = n_freq * PARTS
     depth = len(far_bits)
-    for turn in range(PARTS, count + depth + 1):
+    launched = 2 * PARTS
+    reached = [PARTS] + [0] * depth
+    for turn in range(PARTS, count + AHEAD + depth + 1):
+        while launched < min(count, turn + Z_AHEAD + 1):
+            launch(*divmod(launched, PARTS))
+            launched += 1
         for lag in range(depth + 1):
-            index = turn - lag
-            if lag == 0 and index < count:
-                step, part = divmod(index, PARTS)
-                crossed(step, part).wait_recv()
-                push(step, part, 0)
-            lower = 0 if turn == PARTS else index
-            for slot in range(lower, index + 1):
-                if lag > 0 and 0 <= slot < count:
-                    step, part = divmod(slot, PARTS)
+            limit = min(count, turn + 1 - (lag + AHEAD if lag else 0))
+            for slot in range(reached[lag], limit):
+                step, part = divmod(slot, PARTS)
+                if lag == 0:
+                    crossed(step, part).wait_recv()
+                    push(step, part, 0)
+                else:
                     for mask in far_masks:
                         if bin(mask).count("1") == lag:
                             arrival(step, part, mask).wait_recv()
                             push(step, part, mask)
+            reached[lag] = max(reached[lag], limit)
+    assert min(reached) == count and launched == count
 
     for slot in range(count):
         step, part = divmod(slot, PARTS)

time: 92.1 us -> 90.7 us (0.985)
    pallas_call x1, Pallas kernels: 82.3 us -> 81.4 us  [shards(): pl.pallas_call(functools.partial(exchange_kernel, n_sta, n_freq), out_sha...]
where the time goes in v3:
time: 90.7 us; the launch traced here: 90.6 us
  Pallas kernels  90.6 us (100%)
    pallas_call x1, Pallas kernels, shards(): pl.pallas_call(functools.partial(exchange_kernel, n_sta, n_freq), out_sha...  81.4 us
    pallas_call x1, Pallas kernels, shards(): pl.pallas_call(functools.partial(gram_kernel, per_step, scale), out_shape...  9.2 us

profile of v3, /device:TPU:1, one launch (start us, length us, event | category | flops | bytes accessed | tf_op | source)
XLA Modules:
  0.0 90.6 jit_solution(6131420854613501104)
XLA Ops:
  0.0 81.4 %spectra_exchange.1.panel = bf16[8,4,4,32,16,128]{5,4,3,2,1,0:T(8,128)(2,1)S(1)} custom-call(bf16[128,32,512]{2,1,0:T(8,128)(2,1)} %records.1, s32[32,128]{1,0:T(8,128)} %bitcast.1, bf16[768,512]{1,0:T(8,128)(2,1)} %constant.2.clone.table), custom_call_target="tpu_custom_call" | custom-call | tf_op jit(solution)/shard_map/spectra_exchange/pallas_call | solution.py:242
  81.4 9.2 %gram.1 = bf16[2,32,128,1024]{3,2,1,0:T(8,128)(2,1)} custom-call(bf16[8,4,4,32,16,128]{5,4,3,2,1,0:T(8,128)(2,1)S(1)} %spectra_exchange.1.panel), custom_call_target="tpu_custom_call" | custom-call | tf_op jit(solution)/shard_map/gram/pallas_call | solution.py:269

commit v4 on v3

v4 whole, which is shorter than its diff:
```python
import functools

import jax
import jax.numpy as jnp
import ml_dtypes
import numpy as np
from jax import lax
from jax.experimental import pallas as pl
from jax.experimental.pallas import tpu as pltpu
from jax.sharding import PartitionSpec as P

FFT_LEN = 512
BINS = 128
BAND_LO = 16
PARTS = 4
TERMS = 3
LOADS = 2
HALVES = 2
AHEAD = 2
Z_AHEAD = 6
MESH = pl.DeviceIdType.MESH
MIB = 1 << 20


def spectra_tables():
    t = np.arange(FFT_LEN)
    window = 0.5 - 0.5 * np.cos(2.0 * np.pi * t / FFT_LEN)
    phase = (np.arange(BAND_LO, BAND_LO + BINS)[:, None] * t[None, :] % FFT_LEN) * (2.0 * np.pi / FFT_LEN)
    table = np.concatenate([np.cos(phase), -np.sin(phase)], axis=0) * window
    terms = []
    for _ in range(TERMS):
        terms.append(table.astype(ml_dtypes.bfloat16))
        table = table - terms[-1].astype(np.float64)
    return np.concatenate(terms, axis=0)


def exchange_kernel(
    n_sta, n_freq,
    scale, records, available, table, gathered, early,
    rec, avail, terms, wide, spread, own, rec_sem, keep_sem, zsend, zrecv, send, recv,
):
    me = lax.axis_index("sta")
    z = lax.axis_index("freq")
    stations, load_segs = rec.shape[1], rec.shape[2]
    part_segs = load_segs * LOADS // PARTS
    rows = 2 * part_segs
    bins = BINS // n_freq
    half_bins = bins // HALVES
    mask_bits = [1 << k for k in range(n_sta.bit_length() - 1)]
    far_bits = mask_bits[1:]

    loads = [pltpu.make_async_copy(table, terms, rec_sem.at[LOADS])]
    loads.append(pltpu.make_async_copy(available, avail, rec_sem.at[LOADS + 1]))
    for k in range(LOADS):
        source = records.at[:, pl.ds(k * load_segs, load_segs), :]
        loads.append(pltpu.make_async_copy(source, rec.at[k], rec_sem.at[k]))
    for load in loads:
        load.start()

    barrier = pltpu.get_barrier_semaphore()
    for bit in mask_bits:
        pl.semaphore_signal(barrier, inc=1, device_id=(me ^ bit, z), device_id_type=MESH)
    for step in range(1, n_freq):
        pl.semaphore_signal(barrier, inc=1, device_id=(me, z ^ step), device_id_type=MESH)

    def widen(k):
        def some(block, carry):
            first = pl.multiple_of(block * 16, 16)
            for col in range(FFT_LEN // 128):
                values = rec[k, pl.ds(first, 16), :, pl.ds(col * 128, 128)]
                wide[col, pl.ds(pl.multiple_of(first * load_segs, 256), 16 * load_segs), :] = (
                    values.astype(jnp.float32).reshape(16 * load_segs, 128)
                )
            return carry

        lax.fori_loop(0, stations // 16, some, 0)

    def transform(part):
        offset = part * part_segs % load_segs
        for pair in range(part_segs // 2):
            pieces = []
            for seg in (2 * pair, 2 * pair + 1):
                pieces.append(jnp.concatenate(
                    [wide[col, pl.ds(offset + seg, stations, stride=load_segs), :] for col in range(FFT_LEN // 128)],
                    axis=1,
                ))
            x = jnp.concatenate(pieces, axis=0).astype(jnp.bfloat16)
            contract = (((1,), (1,)), ((), ()))
            sums = lax.dot_general(terms[...], x, contract, preferred_element_type=jnp.float32)
            spectra = sums[(TERMS - 1) * 2 * BINS:]
            for term in range(TERMS - 2, -1, -1):
                spectra = spectra + sums[term * 2 * BINS:(term + 1) * 2 * BINS]
            power = jnp.sum(spectra * spectra, axis=0, keepdims=True) * (1.0 / BINS)
            for k, seg in enumerate((2 * pair, 2 * pair + 1)):
                lanes = slice(k * stations, (k + 1) * stations)
                usable = avail[pl.ds(part * part_segs + seg, 1), :].astype(jnp.float32)
                weight = usable / jnp.sqrt(power[:, lanes] + 1e-05)
                white = spectra[:, lanes] * weight
                spread[pl.ds(seg, BINS, stride=rows), :] = white[:BINS]
                spread[pl.ds(part_segs + seg, BINS, stride=rows), :] = white[BINS:]

        for dest in range(n_freq):
            block = spread[dest * bins * rows:(dest + 1) * bins * rows, :]
            own[dest, :, part] = block.astype(jnp.bfloat16).reshape(HALVES, half_bins, rows, 128)

    chunks = [(0, 0, part, 1) for part in range(PARTS)]
    for half in range(HALVES):
        for step in range(n_freq):
            if (half, step) != (0, 0):
                chunks += [(half, step, part, 2) for part in range(0, PARTS, 2)]
    count = len(chunks)
    first_half = sum(chunk[0] == 0 for chunk in chunks)

    def orders(slot):
        return far_bits if slot % 2 == 0 else far_bits[::-1]

    def piece(slot, mask):
        half, step, part, parts = chunks[slot]
        return gathered.at[me ^ mask, z ^ step, half, pl.ds(part, parts)]

    def forward(slot, mask, bit):
        half, step, part, parts = chunks[slot]
        src = own.at[z, half, pl.ds(part, parts)] if mask == 0 and step == 0 else piece(slot, mask)
        return pltpu.make_async_remote_copy(
            src_ref=src, dst_ref=piece(slot, mask),
            send_sem=send.at[slot, mask ^ bit], recv_sem=recv.at[slot, mask ^ bit],
            device_id=(me ^ bit, z), device_id_type=MESH,
        )

    def arrival(slot, mask):
        here = piece(slot, mask)
        return pltpu.make_async_remote_copy(
            src_ref=here, dst_ref=here, send_sem=send.at[slot, mask], recv_sem=recv.at[slot, mask],
            device_id=(me ^ (mask & -mask), z), device_id_type=MESH,
        )

    def cross(slot):
        half, step, part, parts = chunks[slot]
        return pltpu.make_async_remote_copy(
            src_ref=own.at[z ^ step, half, pl.ds(part, parts)],
            dst_ref=gathered.at[me, z, half, pl.ds(part, parts)],
            send_sem=zsend.at[slot], recv_sem=zrecv.at[slot],
            device_id=(me, z ^ step), device_id_type=MESH,
        )

    def crossed(slot):
        here = piece(slot, 0)
        return pltpu.make_async_remote_copy(
            src_ref=here, dst_ref=here, send_sem=zsend.at[slot], recv_sem=zrecv.at[slot],
            device_id=(me, z ^ chunks[slot][1]), device_id_type=MESH,
        )

    started = []

    def push(slot, mask):
        order = orders(slot)
        last = max([order.index(bit) for bit in order if mask & bit], default=-1)
        for bit in order[last + 1:] + [1]:
            copy = forward(slot, mask, bit)
            copy.start()
            started.append(copy)

    def launch(slot):
        copy = cross(slot)
        copy.start()
        started.append(copy)

    keeps = []
    for part in range(PARTS):
        if part == 0:
            loads[0].wait()
            loads[1].wait()
        if part % (PARTS // LOADS) == 0:
            loads[2 + part * LOADS // PARTS].wait()
            widen(part * LOADS // PARTS)
        transform(part)
        if part == 0:
            pl.semaphore_wait(barrier, len(mask_bits) + n_freq - 1)
        push(part, 0)
        if part % 2 == 1:
            launch(PARTS + part // 2)
        keep = pltpu.make_async_copy(own.at[z, :, part], gathered.at[me, z, :, part], keep_sem.at[part])
        keep.start()
        keeps.append(keep)

    def early_bins(start, stop):
        def one(b, carry):
            gram_bin(
                me, scale, n_sta, n_freq,
                lambda j, zz, part: gathered[j, zz, 0, part, b],
                lambda k, columns, value: early.__setitem__((k, b, slice(None), columns), value),
            )
            return carry

        lax.fori_loop(start, stop, one, 0)

    far_masks = [mask for mask in range(2, n_sta, 2)]
    depth = len(far_bits)
    launched = PARTS + PARTS // 2
    reached = [PARTS] + [0] * depth
    done_bins, turns = None, count + AHEAD + depth + 1
    for turn in range(PARTS, turns):
        while launched < min(count, turn + Z_AHEAD + 1):
            if chunks[launched][1] > 0:
                launch(launched)
            launched += 1
        for lag in range(depth + 1):
            limit = min(count, turn + 1 - (lag + AHEAD if lag else 0))
            for slot in range(reached[lag], limit):
                if lag == 0:
                    if chunks[slot][1] > 0:
                        crossed(slot).wait_recv()
                    push(slot, 0)
                else:
                    for mask in far_masks:
                        if bin(mask).count("1") == lag:
                            arrival(slot, mask).wait_recv()
                            push(slot, mask)
            reached[lag] = max(reached[lag], limit)
        if done_bins is not None and done_bins < half_bins:
            stop = min(half_bins, done_bins + 2)
            early_bins(done_bins, stop)
            done_bins = stop
        if done_bins is None and min(reached) >= first_half:
            for slot in range(first_half):
                for mask in range(1, n_sta, 2):
                    arrival(slot, mask).wait_recv()
            for keep in keeps:
                keep.wait()
            done_bins = 0
    assert min(reached) == count and launched == count
    if done_bins < half_bins:
        early_bins(done_bins, half_bins)

    for slot in range(first_half, count):
        for mask in range(1, n_sta, 2):
            arrival(slot, mask).wait_recv()
    for copy in started:
        copy.wait_send()


def gram_bin(me, scale, n_sta, n_freq, block_of, write):
    places = [(z, part) for z in range(n_freq) for part in range(PARTS)]
    plain, turned = [], []
    for z, part in places:
        block = block_of(me, z, part).astype(jnp.float32) * scale
        half = block.shape[0] // 2
        plain.append(block)
        turned += [block[half:], -block[:half]]
    mine = jnp.concatenate([jnp.concatenate(plain, axis=0), jnp.concatenate(turned, axis=0)], axis=1)
    mine = mine.T.astype(jnp.bfloat16)
    stations = mine.shape[0] // 2
    for j in range(0, n_sta, 2):
        other = jnp.concatenate(
            [jnp.concatenate([block_of(j + k, z, part) for z, part in places], axis=0) for k in (0, 1)], axis=1
        )
        gram = jnp.dot(mine, other, preferred_element_type=jnp.float32).astype(jnp.bfloat16)
        columns = slice(j * stations, (j + 2) * stations)
        write(0, columns, gram[:stations])
        write(1, columns, gram[stations:])


def gram_kernel(per_step, scale, panel, early, out):
    me = lax.axis_index("sta")
    n_sta, n_freq = panel.shape[:2]
    first = pl.program_id(0) * per_step
    for b in range(per_step):
        for k in range(2):
            out[k, 0, b] = early[k, first + b]
        gram_bin(
            me, scale, n_sta, n_freq,
            lambda j, z, part: panel[j, z, 1, part, first + b],
            lambda k, columns, value: out.__setitem__((k, 1, b, slice(None), columns), value),
        )


def shards(n_sta, n_freq, records, available):
    stations, segments, samples = records.shape
    part_segs = segments // PARTS
    rows = 2 * part_segs
    bins = BINS // n_freq
    operands = [records, available.T, jnp.asarray(spectra_tables())]
    operands = [pltpu.with_memory_space_constraint(operand, pltpu.HBM) for operand in operands]
    half_bins = bins // HALVES
    scale = 1.0 / (segments * n_freq)
    count = HALVES * n_freq * PARTS // 2 + PARTS // 2
    gathered, early = pl.pallas_call(
        functools.partial(exchange_kernel, n_sta, n_freq, scale),
        out_shape=(
            jax.ShapeDtypeStruct((n_sta, n_freq, HALVES, PARTS, half_bins, rows, stations), jnp.bfloat16),
            jax.ShapeDtypeStruct((2, half_bins, stations, stations * n_sta), jnp.bfloat16),
        ),
        in_specs=[pl.BlockSpec(memory_space=pltpu.HBM)] * len(operands),
        out_specs=[pl.BlockSpec(memory_space=pltpu.VMEM)] * 2,
        scratch_shapes=[
            pltpu.VMEM((LOADS, stations, segments // LOADS, samples), jnp.bfloat16),
            pltpu.VMEM((segments, stations), jnp.int32),
            pltpu.VMEM((TERMS * 2 * BINS, samples), jnp.bfloat16),
            pltpu.VMEM((samples // 128, stations * segments // LOADS, 128), jnp.float32),
            pltpu.VMEM((BINS * rows, stations), jnp.float32),
            pltpu.VMEM((n_freq, HALVES, PARTS, half_bins, rows, stations), jnp.bfloat16),
            pltpu.SemaphoreType.DMA((LOADS + 2,)),
            pltpu.SemaphoreType.DMA((PARTS,)),
            pltpu.SemaphoreType.DMA((count,)),
            pltpu.SemaphoreType.DMA((count,)),
            pltpu.SemaphoreType.DMA((count, n_sta)),
            pltpu.SemaphoreType.DMA((count, n_sta)),
        ],
        compiler_params=pltpu.CompilerParams(
            collective_id=0, has_side_effects=True, vmem_limit_bytes=13 * MIB
        ),
        name="spectra_exchange",
    )(*operands)

    per_step = 2
    wide = stations * n_sta
    gram = pl.pallas_call(
        functools.partial(gram_kernel, per_step, scale),
        out_shape=jax.ShapeDtypeStruct((2, HALVES, half_bins, stations, wide), jnp.bfloat16),
        grid=(half_bins // per_step,),
        in_specs=[pl.BlockSpec(memory_space=pltpu.VMEM)] * 2,
        out_specs=pl.BlockSpec((2, HALVES, per_step, stations, wide), lambda i: (0, 0, i, 0, 0)),
        compiler_params=pltpu.CompilerParams(vmem_limit_bytes=11 * MIB),
        name="gram",
    )(gathered, early)
    return gram.reshape(2, bins, stations, wide)


def solution(mesh):
    in_specs = (P("sta", "freq", None), P("sta", "freq"))
    out_specs = P(None, "freq", "sta", None)
    body = functools.partial(shards, mesh.shape["sta"], mesh.shape["freq"])
    return jax.shard_map(body, mesh=mesh, in_specs=in_specs, out_specs=out_specs, check_vma=False)
```

time: 90.7 us -> 100 us (1.10)
  Pallas kernels: 90.6 us -> 99.8 us
    pallas_call x1, Pallas kernels: 81.4 us -> 91.4 us  [shards(): pl.pallas_call(functools.partial(exchange_kernel, n_sta, n_freq, scale),...]
where the time goes in v4:
time: 100 us; the launch traced here: 99.8 us
  Pallas kernels  99.8 us (100%)
    pallas_call x1, Pallas kernels, shards(): pl.pallas_call(functools.partial(exchange_kernel, n_sta, n_freq, scale),...  91.4 us
    pallas_call x1, Pallas kernels, shards(): pl.pallas_call(functools.partial(gram_kernel, per_step, scale), out_shape...  8.45 us

profile of v4, /device:TPU:1, one launch (start us, length us, event | category | flops | bytes accessed | tf_op | source)
XLA Modules:
  0.0 99.8 jit_solution(2954149327340852913)
XLA Ops:
  0.0 91.4 %spectra_exchange.1 = (bf16[8,4,2,4,16,16,128]{6,5,4,3,2,1,0:T(8,128)(2,1)S(1)}, bf16[2,16,128,1024]{3,2,1,0:T(8,128)(2,1)S(1)}) custom-call(bf16[128,32,512]{2,1,0:T(8,128)(2,1)} %records.1, s32[32,128]{1,0:T(8,128)} %bitcast.2, bf16[768,512]{1,0:T(8,128)(2,1)} %constant.2.clone.table), custom_call_target="tpu_custom_call" | custom-call | tf_op jit(solution)/shard_map/spectra_exchange/pallas_call | solution.py:287
  91.4 8.5 %gram.1 = bf16[2,2,16,128,1024]{4,3,2,1,0:T(8,128)(2,1)} custom-call(bf16[8,4,2,4,16,16,128]{6,5,4,3,2,1,0:T(8,128)(2,1)S(1)} %get-tuple-element.7.panel, bf16[2,16,128,1024]{3,2,1,0:T(8,128)(2,1)S(1)} %get-tuple-element.8.early), custom_call_target="tpu_custom_call" | custom-call | tf_op jit(solution)/shard_map/gram/pallas_call | solution.py:317

commit v5 on v3

--- a/solution.py
+++ b/solution.py
@@ -15,7 +15,7 @@
 PARTS = 4
 TERMS = 3
 LOADS = 2
-AHEAD = 2
+AHEAD = 4
 Z_AHEAD = 6
 MESH = pl.DeviceIdType.MESH
 MIB = 1 << 20
@@ -264,7 +264,7 @@
         name="spectra_exchange",
     )(*operands)
 
-    per_step = 4
+    per_step = 2
     scale = 1.0 / (segments * n_freq)
     return pl.pallas_call(
         functools.partial(gram_kernel, per_step, scale),

time: 90.7 us -> 101 us (1.11)
  Pallas kernels: 90.6 us -> 101 us
    pallas_call x1, Pallas kernels: 81.4 us -> 88.9 us  [shards(): pl.pallas_call(functools.partial(exchange_kernel, n_sta, n_freq), out_sha...]
    pallas_call x1, Pallas kernels: 9.2 us -> 12.3 us  [shards(): pl.pallas_call(functools.partial(gram_kernel, per_step, scale), out_shape...]
where the time goes in v5:
time: 101 us
  Pallas kernels  101 us (100%)
    pallas_call x1, Pallas kernels, shards(): pl.pallas_call(functools.partial(exchange_kernel, n_sta, n_freq), out_sha...  88.9 us
    pallas_call x1, Pallas kernels, shards(): pl.pallas_call(functools.partial(gram_kernel, per_step, scale), out_shape...  12.3 us

profile of v5, /device:TPU:1, one launch (start us, length us, event | category | flops | bytes accessed | tf_op | source)
XLA Modules:
  0.0 101.3 jit_solution(13656015285117053259)
XLA Ops:
  0.0 88.9 %spectra_exchange.1.panel = bf16[8,4,4,32,16,128]{5,4,3,2,1,0:T(8,128)(2,1)S(1)} custom-call(bf16[128,32,512]{2,1,0:T(8,128)(2,1)} %records.1, s32[32,128]{1,0:T(8,128)} %bitcast.1, bf16[768,512]{1,0:T(8,128)(2,1)} %constant.2.clone.table), custom_call_target="tpu_custom_call" | custom-call | tf_op jit(solution)/shard_map/spectra_exchange/pallas_call | solution.py:242
  88.9 12.3 %gram.1 = bf16[2,32,128,1024]{3,2,1,0:T(8,128)(2,1)} custom-call(bf16[8,4,4,32,16,128]{5,4,3,2,1,0:T(8,128)(2,1)S(1)} %spectra_exchange.1.panel), custom_call_target="tpu_custom_call" | custom-call | tf_op jit(solution)/shard_map/gram/pallas_call | solution.py:269
